TPU v7x, 512 devices: a whole 4x8x8 slice. The times are simulated.
512 devices in a mesh: inst: 2 (over y_hi), blk: 256 (over z, y_lo, x, core).
Axes of the slice: x: 4, y: 8 (y_hi: 2, y_lo: 4; y = y_hi * 4 + y_lo), z: 8, core: 2. Of those that a mesh axis runs over, the one named last changes fastest.
Arguments:
- state: float32 [8, 5, 256, 32, 256], P('inst', None, 'blk'), as said below
- slot_of: int32 [256], replicated, may hold values from 0 to 255, as said below
- conn_block: int32 [256, 2], replicated, may hold values from 0 to 255, as said below
- conn_side: int32 [256, 2], replicated, may hold values from 0 to 1
- conn_shift: int32 [256, 2], replicated, may hold values from 0 to 255
- rows: int32 [256], replicated, may hold values from 16 to 32
Outputs:
- residual: float32 [8, 5, 256, 32, 256], P('inst', None, 'blk')
Inputs may be any that keep to these rules, and one draw needn't show every extreme that they name: slot_of is a permutation of the block numbers. With d(b) = slot_of[b], the index along blk of the device holding block b, d(conn_block[b, f]) - d(b) taken cyclically modulo the number of blk devices lies within -2 to 2; both ends are reached in every draw. `state`: density and pressure are positive.
All inputs are finite; a program needn't handle non-finite values.
Results may differ from a plain program's by a relative error of at most 0.00012.
Values sent between devices are 32-bit elements; how exact they have to be, the bound alone decides.
A program may use at most 64 MiB of HBM per device.

v0:
```python
import math

import jax
import jax.numpy as jnp
from jax import lax
from jax.sharding import PartitionSpec as P

REACH = 2


GAMMA_MINUS = 0.4
DAMPING = 0.05
FREQUENCY = 1.0


def passed_along(value, axis, steps):
    count = lax.axis_size(axis)
    pairs = [(source, (source + steps) % count) for source in range(count)]
    return lax.ppermute(value, axis, pairs)


def spectral_matrix(count):
    position = jnp.arange(count, dtype=jnp.int32)
    offset = position[:, None] - position[None, :]
    angle = math.pi / count * offset.astype(jnp.float32)
    safe_sin = jnp.where(offset == 0, 1.0, jnp.sin(angle))
    parity = 1.0 - 2.0 * jnp.mod(offset, 2).astype(jnp.float32)
    return jnp.where(offset == 0, 0.0, 0.5 * FREQUENCY * parity * jnp.cos(angle) / safe_sin)


def euler_flux(fields, direction):
    density = fields[:, 0]
    momentum_x = fields[:, 1]
    momentum_y = fields[:, 2]
    momentum_z = fields[:, 3]
    energy = fields[:, 4]
    pressure = GAMMA_MINUS * (
        energy
        - 0.5
        * (momentum_x * momentum_x + momentum_y * momentum_y + momentum_z * momentum_z)
        / density
    )
    velocity = fields[:, direction] / density
    parts = [
        fields[:, direction],
        momentum_x * velocity,
        momentum_y * velocity,
        momentum_z * velocity,
        (energy + pressure) * velocity,
    ]
    parts[direction] = parts[direction] + pressure
    return jnp.stack(parts, axis=1)


def edge_rows(state, my_rows):
    low = state[:, :, :, 0:2]
    upper = lax.dynamic_slice_in_dim(state[:, :, 0], my_rows[0] - 2, 2, 2)
    highs = [upper[:, :, ::-1]]
    high = jnp.stack(highs, axis=2)
    return jnp.stack([low, high], axis=3)


def pick_ghosts(all_rims, local_slot, nb_side, shift):
    faces = []
    for face in range(2):
        taken = lax.dynamic_index_in_dim(all_rims, local_slot[0, face], 2, keepdims=False)
        taken = lax.dynamic_index_in_dim(taken, nb_side[0, face], 2, keepdims=False)
        faces.append(jnp.roll(taken, -shift[0, face], axis=3))
    per_block = [jnp.stack(faces, axis=2)]
    return jnp.stack(per_block, axis=2)


def spatial_residual(fields, ghosts, block_rows):
    row_count = fields.shape[3]
    stacked = jnp.concatenate([ghosts[:, :, :, 0, ::-1], fields, fields[:, :, :, -2:]], axis=3)
    offset = jnp.arange(row_count + 4, dtype=jnp.int32)[None, :] - 2 - block_rows[:, None]
    first_layer = (offset == 0)[None, None, :, :, None]
    second_layer = (offset == 1)[None, None, :, :, None]
    extended = jnp.where(
        first_layer,
        ghosts[:, :, :, 1, 0][:, :, :, None],
        jnp.where(second_layer, ghosts[:, :, :, 1, 1][:, :, :, None], stacked),
    )
    flux_rows = euler_flux(extended, 1)
    slope_rows = (
        8.0 * (flux_rows[:, :, :, 3:-1] - flux_rows[:, :, :, 1:-3])
        - (flux_rows[:, :, :, 4:] - flux_rows[:, :, :, :-4])
    ) / 12.0
    smooth_rows = (
        extended[:, :, :, 4:]
        - 4.0 * extended[:, :, :, 3:-1]
        + 6.0 * extended[:, :, :, 2:-2]
        - 4.0 * extended[:, :, :, 1:-3]
        + extended[:, :, :, :-4]
    )
    flux_cols = euler_flux(fields, 2)
    slope_cols = (
        8.0 * (jnp.roll(flux_cols, -1, 4) - jnp.roll(flux_cols, 1, 4))
        - (jnp.roll(flux_cols, -2, 4) - jnp.roll(flux_cols, 2, 4))
    ) / 12.0
    smooth_cols = (
        jnp.roll(fields, -2, 4)
        - 4.0 * jnp.roll(fields, -1, 4)
        + 6.0 * fields
        - 4.0 * jnp.roll(fields, 1, 4)
        + jnp.roll(fields, 2, 4)
    )
    return -(slope_rows + slope_cols) - DAMPING * (smooth_rows + smooth_cols)


def on_device(state, slot_of, conn_block, conn_side, conn_shift, rows):
    inst_dev = state.shape[0]
    blk_dev = state.shape[2]
    row_count = state.shape[3]
    blocks = slot_of.shape[0]
    ids_of_slot = (
        jnp.zeros((blocks,), jnp.int32).at[slot_of].set(jnp.arange(blocks, dtype=jnp.int32))
    )
    blk_place = lax.axis_index("blk")
    my_slots = blk_place * blk_dev + jnp.arange(blk_dev, dtype=jnp.int32)
    my_ids = ids_of_slot[my_slots]
    my_rows = rows[my_ids]
    boundary = edge_rows(state, my_rows)
    nb_slots = slot_of[conn_block[my_ids]]
    blk_span = lax.axis_size("blk")
    pieces = []
    for window in range(2 * REACH + 1):
        if window == REACH:
            pieces.append(boundary)
        else:
            pieces.append(passed_along(boundary, "blk", REACH - window))
    all_rims = jnp.concatenate(pieces, axis=2)
    distance = jnp.mod(nb_slots // blk_dev - blk_place + REACH, blk_span)
    local_slot = distance * blk_dev + jnp.mod(nb_slots, blk_dev)
    ghosts = pick_ghosts(all_rims, local_slot, conn_side[my_ids], conn_shift[my_ids])
    spatial = spatial_residual(state, ghosts, my_rows)
    cycle_size = lax.axis_size("inst")
    cycle_place = lax.axis_index("inst")
    derivative = spectral_matrix(inst_dev * cycle_size)
    own_rows = lax.dynamic_slice_in_dim(derivative, cycle_place * inst_dev, inst_dev, 0)
    all_states = lax.all_gather(state, "inst", axis=0, tiled=True)
    source = jnp.einsum("nm,mvbij->nvbij", own_rows, all_states, precision=lax.Precision.HIGHEST)
    inside = (jnp.arange(row_count, dtype=jnp.int32)[None, :] < my_rows[:, None])[
        None, None, :, :, None
    ]
    return jnp.where(inside, spatial - source, 0.0)


def solution(mesh):
    in_specs = (P("inst", None, "blk", None, None), P(), P(), P(), P(), P())
    out_specs = P("inst", None, "blk", None, None)
    return jax.shard_map(
        on_device, mesh=mesh, in_specs=in_specs, out_specs=out_specs, check_vma=False
    )
```

profile of v0, /device:TPU:9, one launch (start us, length us, event | category | flops | bytes accessed | tf_op | source)
XLA Modules:
  0.0 100.8 jit_solution(9239169802677168952)
XLA Ops:
  6.6 0.7 compare_select_fusion
  7.3 1.4 %scatter_custom_fusion = s32[256]{0:T(256)S(1)} fusion(s32[256]{0:T(256)S(1)} %compare_select_fusion, s32[256]{0:T(256)S(1)} %iota.25, s32[]{:T(128)} %constant.170.clone.1), kind=kCustom, calls=%fused_computation.104 | custom fusion | bytes 1028 | tf_op jit(solution)/shard_map/scatter | solution.py:117
  8.7 0.7 dynamic-slice.18
  11.5 1.3 %dynamic-slice.19 = s32[1]{0:T(128)} dynamic-slice(s32[256]{0:T(256)} %param.13, s32[]{:T(128)} %bitcast.2), dynamic_slice_sizes={1} | dynamic-slice | bytes 12 | tf_op jit(solution)/shard_map/gather | solution.py:122
  13.9 1.1 %slice_bitcast_fusion = (f32[4,5,1,1,2,256]{5,4,1,0,3,2:T(2,128)S(1)}, f32[4,5,2,256]{3,2,1,0:T(2,128)S(1)}) fusion(f32[4,5,1,32,256]{4,3,2,1,0:T(8,128)} %param.8, s32[]{:T(128)S(6)} %select_n.131), kind=kLoop, calls=%fused_computation.65 | loop fusion | bytes 163844 | tf_op jit(solution)/shard_map/stack | solution.py:60
  15.2 3.1 %collective-permute-start = (f32[4,5,1,2,2,256]{5,4,1,0,3,2:T(2,128)S(1)}, f32[4,5,1,2,2,256]{5,4,1,0,3,2:T(2,128)S(1)}, u32[]{:S(2)}, u32[]{:S(2)}) collective-permute-start(f32[4,5,1,2,2,256]{5,4,1,0,3,2:T(2,128)S(1)} %pad_maximum_fusion), channel_id=1, source_target_pairs={{0,2},{1,3},{2,4},{3,5},{4,6},{5,7},{6,8},{7,9},{8,10},{9,11},{10,... | collective-permute-start | bytes 245768 | tf_op jit(solution)/shard_map/ppermute | solution.py:19
  18.3 4.0 %collective-permute-start.1 = (f32[4,5,1,2,2,256]{5,4,1,0,3,2:T(2,128)S(1)}, f32[4,5,1,2,2,256]{5,4,1,0,3,2:T(2,128)S(1)}, u32[]{:S(2)}, u32[]{:S(2)}) collective-permute-start(f32[4,5,1,2,2,256]{5,4,1,0,3,2:T(2,128)S(1)} %pad_maximum_fusion), channel_id=1, source_target_pairs={{0,1},{1,2},{2,3},{3,4},{4,5},{5,6},{6,7},{7,8},{8,9},{9,10},{10,1... | collective-permute-start | bytes 245768 | tf_op jit(solution)/shard_map/ppermute | solution.py:19
  22.3 1.9 %collective-permute-start.2 = (f32[4,5,1,2,2,256]{5,4,1,0,3,2:T(2,128)S(1)}, f32[4,5,1,2,2,256]{5,4,1,0,3,2:T(2,128)S(1)}, u32[]{:S(2)}, u32[]{:S(2)}) collective-permute-start(f32[4,5,1,2,2,256]{5,4,1,0,3,2:T(2,128)S(1)} %pad_maximum_fusion), channel_id=1, source_target_pairs={{0,255},{1,0},{2,1},{3,2},{4,3},{5,4},{6,5},{7,6},{8,7},{9,8},{10,... | collective-permute-start | bytes 245768 | tf_op jit(solution)/shard_map/ppermute | solution.py:19
  24.3 4.3 %collective-permute-start.3 = (f32[4,5,1,2,2,256]{5,4,1,0,3,2:T(2,128)S(1)}, f32[4,5,1,2,2,256]{5,4,1,0,3,2:T(2,128)S(1)}, u32[]{:S(2)}, u32[]{:S(2)}) collective-permute-start(f32[4,5,1,2,2,256]{5,4,1,0,3,2:T(2,128)S(1)} %pad_maximum_fusion), channel_id=1, source_target_pairs={{0,254},{1,255},{2,0},{3,1},{4,2},{5,3},{6,4},{7,5},{8,6},{9,7},{1... | collective-permute-start | bytes 245768 | tf_op jit(solution)/shard_map/ppermute | solution.py:19
  29.4 0.7 fusion.62
  39.7 1.5 %fusion.59 = (f32[4,5,1,32,255]{4,0,3,1,2:T(4,128)}, f32[4,5,1,32,255]{4,0,3,1,2:T(4,128)}) fusion(f32[4,5,1,32,256]{4,0,3,1,2:T(4,128)S(1)} %multiply_dynamic-update-slice_fusion.3), kind=kLoop, calls=%fused_computation.116 | loop fusion | bytes 2611200 | tf_op jit(solution)/shard_map/jit(_roll_static)/slice | solution.py:98
  41.3 1.1 %fusion.56 = (f32[4,5,1,32,2]{4,0,3,1,2:T(4,128)}, f32[4,5,1,32,2]{4,0,3,1,2:T(4,128)}) fusion(f32[4,5,1,32,256]{4,0,3,1,2:T(4,128)S(1)} %multiply_dynamic-update-slice_fusion.3), kind=kLoop, calls=%fused_computation.113 | loop fusion | bytes 20480 | tf_op jit(solution)/shard_map/jit(_roll_static)/slice | solution.py:99
  42.3 1.0 %fusion.58 = (f32[4,5,1,32,1]{4,0,3,1,2:T(4,128)}, f32[4,5,1,32,1]{4,0,3,1,2:T(4,128)}) fusion(f32[4,5,1,32,256]{4,0,3,1,2:T(4,128)S(1)} %multiply_dynamic-update-slice_fusion.3), kind=kLoop, calls=%fused_computation.115 | loop fusion | bytes 10240 | tf_op jit(solution)/shard_map/jit(_roll_static)/slice | solution.py:98
  43.3 1.5 %fusion.53 = (f32[4,5,1,32,254]{4,0,3,1,2:T(4,128)}, f32[4,5,1,32,254]{4,0,3,1,2:T(4,128)}) fusion(f32[4,5,1,32,256]{4,0,3,1,2:T(4,128)S(1)} %copy.48), kind=kLoop, calls=%fused_computation.110 | loop fusion | bytes 2600960 | tf_op jit(solution)/shard_map/jit(_roll_static)/slice | solution.py:106
  44.9 1.5 %fusion.55 = (f32[4,5,1,32,255]{4,0,3,1,2:T(4,128)}, f32[4,5,1,32,255]{4,0,3,1,2:T(4,128)}) fusion(f32[4,5,1,32,256]{4,0,3,1,2:T(4,128)S(1)} %copy.48), kind=kLoop, calls=%fused_computation.112 | loop fusion | bytes 2611200 | tf_op jit(solution)/shard_map/jit(_roll_static)/slice | solution.py:105
  46.4 1.1 %fusion.52 = (f32[4,5,1,32,2]{4,0,3,1,2:T(4,128)}, f32[4,5,1,32,2]{4,0,3,1,2:T(4,128)}) fusion(f32[4,5,1,32,256]{4,0,3,1,2:T(4,128)S(1)} %copy.48), kind=kLoop, calls=%fused_computation.109 | loop fusion | bytes 20480 | tf_op jit(solution)/shard_map/jit(_roll_static)/slice | solution.py:106
  47.5 1.1 %fusion.54 = (f32[4,5,1,32,1]{4,0,3,1,2:T(4,128)}, f32[4,5,1,32,1]{4,0,3,1,2:T(4,128)}) fusion(f32[4,5,1,32,256]{4,0,3,1,2:T(4,128)S(1)} %copy.48), kind=kLoop, calls=%fused_computation.111 | loop fusion | bytes 10240 | tf_op jit(solution)/shard_map/jit(_roll_static)/slice | solution.py:105
  53.5 0.8 add_dynamic-update-slice_fusion
  54.2 0.7 multiply_dynamic-update-slice_fusion.2
  54.9 0.7 multiply_dynamic-update-slice_fusion.1
  55.6 0.7 multiply_dynamic-update-slice_fusion
  56.4 28.9 %all-gather.2.cloned.1.call-done = f32[8,5,1,32,256]{4,3,2,1,0:T(8,128)} async-done(((f32[4,5,1,32,256]{4,3,2,1,0:T(8,128)}), f32[8,5,1,32,256]{4,3,2,1,0:T(8,128)}) %all-gather.2.cloned.1.call-update) | async-done | bytes 1310736 | tf_op jit(solution)/shard_map/all_gather | solution.py:141
  85.3 7.7 %fusion.9 = f32[4,5,1,32,256]{4,0,3,1,2:T(4,128)S(1)} fusion(f32[8,5,1,32,256]{4,3,2,1,0:T(8,128)} %all-gather.2.cloned.1.call-done, f32[4,5,1,36,256]{4,0,3,1,2:T(4,128)S(1)} %fusion.12, f32[4,5,1,36,256]{4,0,3,1,2:T(4,128)} %multiply_dynamic-update-slice_fusion, f32[4,5,1,32,1]{4,0,3,1,2:T(4,128)} %get-tuple-element.81, ...), kind=kOutput, calls=%fused_computation.7 | convolution fusion | flops 21954560 | bytes 13775364 | tf_op jit(solution)/shard_map/nm,mvbij->nvbij/dot_general | solution.py:142
  93.0 1.0 copy.64
  (59 shorter events, 6.3 us)
Async XLA Ops:
  6.5 22.0 %copy-start = (s32[256,2]{0,1:T(2,128)S(1)}, s32[256,2]{0,1:T(2,128)}, u32[]{:S(2)}) copy-start(s32[256,2]{0,1:T(2,128)} %param.10) | copy-start | bytes 6148
  6.5 22.2 %copy-start.1 = (s32[256]{0:T(256)S(1)}, s32[256]{0:T(256)}, u32[]{:S(2)}) copy-start(s32[256]{0:T(256)} %param.9) | copy-start | bytes 3076
  6.5 31.9 %copy-start.4 = (f32[4,5,1,32,256]{4,3,2,1,0:T(8,128)S(1)}, f32[4,5,1,32,256]{4,3,2,1,0:T(8,128)}, u32[]{:S(2)}) copy-start(f32[4,5,1,32,256]{4,3,2,1,0:T(8,128)} %param.8) | copy-start | bytes 1966084
  6.5 26.1 %copy-start.6 = (s32[256,2]{0,1:T(2,128)S(1)}, s32[256,2]{0,1:T(2,128)}, u32[]{:S(2)}) copy-start(s32[256,2]{0,1:T(2,128)} %param.11) | copy-start | bytes 6148
  6.5 26.1 %copy-start.5 = (s32[256,2]{0,1:T(2,128)S(1)}, s32[256,2]{0,1:T(2,128)}, u32[]{:S(2)}) copy-start(s32[256,2]{0,1:T(2,128)} %param.12) | copy-start | bytes 6148
  6.5 78.8 %all-gather.2.cloned.1.call-start = ((), (), s32[]{:S(2)}) async-start(), calls=%async_computation | async-start | bytes 1966080 | tf_op jit(solution)/shard_map/all_gather | solution.py:141
  15.2 36.6 %collective-permute-start = (f32[4,5,1,2,2,256]{5,4,1,0,3,2:T(2,128)S(1)}, f32[4,5,1,2,2,256]{5,4,1,0,3,2:T(2,128)S(1)}, u32[]{:S(2)}, u32[]{:S(2)}) collective-permute-start(f32[4,5,1,2,2,256]{5,4,1,0,3,2:T(2,128)S(1)} %pad_maximum_fusion), channel_id=1, source_target_pairs={{0,2},{1,3},{2,4},{3,5},{4,6},{5,7},{6,8},{7,9},{8,10},{9,11},{10,... | collective-permute-start | bytes 245768 | tf_op jit(solution)/shard_map/ppermute | solution.py:19
  18.3 33.6 %collective-permute-start.1 = (f32[4,5,1,2,2,256]{5,4,1,0,3,2:T(2,128)S(1)}, f32[4,5,1,2,2,256]{5,4,1,0,3,2:T(2,128)S(1)}, u32[]{:S(2)}, u32[]{:S(2)}) collective-permute-start(f32[4,5,1,2,2,256]{5,4,1,0,3,2:T(2,128)S(1)} %pad_maximum_fusion), channel_id=1, source_target_pairs={{0,1},{1,2},{2,3},{3,4},{4,5},{5,6},{6,7},{7,8},{8,9},{9,10},{10,1... | collective-permute-start | bytes 245768 | tf_op jit(solution)/shard_map/ppermute | solution.py:19
  22.3 29.6 %collective-permute-start.2 = (f32[4,5,1,2,2,256]{5,4,1,0,3,2:T(2,128)S(1)}, f32[4,5,1,2,2,256]{5,4,1,0,3,2:T(2,128)S(1)}, u32[]{:S(2)}, u32[]{:S(2)}) collective-permute-start(f32[4,5,1,2,2,256]{5,4,1,0,3,2:T(2,128)S(1)} %pad_maximum_fusion), channel_id=1, source_target_pairs={{0,255},{1,0},{2,1},{3,2},{4,3},{5,4},{6,5},{7,6},{8,7},{9,8},{10,... | collective-permute-start | bytes 245768 | tf_op jit(solution)/shard_map/ppermute | solution.py:19
  24.3 27.7 %collective-permute-start.3 = (f32[4,5,1,2,2,256]{5,4,1,0,3,2:T(2,128)S(1)}, f32[4,5,1,2,2,256]{5,4,1,0,3,2:T(2,128)S(1)}, u32[]{:S(2)}, u32[]{:S(2)}) collective-permute-start(f32[4,5,1,2,2,256]{5,4,1,0,3,2:T(2,128)S(1)} %pad_maximum_fusion), channel_id=1, source_target_pairs={{0,254},{1,255},{2,0},{3,1},{4,2},{5,3},{6,4},{7,5},{8,6},{9,7},{1... | collective-permute-start | bytes 245768 | tf_op jit(solution)/shard_map/ppermute | solution.py:19
  38.9 8.5 %copy-start.2 = (f32[4,5,1,32,256]{4,0,3,1,2:T(4,128)}, f32[4,5,1,32,256]{4,0,3,1,2:T(4,128)S(1)}, u32[]{:S(2)}) copy-start(f32[4,5,1,32,256]{4,0,3,1,2:T(4,128)S(1)} %copy.48) | copy-start | bytes 1966084
  48.5 4.0 %copy-start.3 = (f32[4,5,1,32,256]{4,0,3,1,2:T(4,128)S(1)}, f32[4,5,1,32,256]{4,0,3,1,2:T(4,128)}, u32[]{:S(2)}) copy-start(f32[4,5,1,32,256]{4,0,3,1,2:T(4,128)} %copy-done.2) | copy-start | bytes 1966084
  48.6 4.0 %slice-start = ((f32[4,5,1,32,256]{4,0,3,1,2:T(4,128)}), f32[4,5,1,2,256]{4,0,3,1,2:T(4,128)S(1)}, s32[]{:S(2)}) async-start(f32[4,5,1,32,256]{4,0,3,1,2:T(4,128)} %copy-done.2), calls=%async_computation.1 | async-start | bytes 81920 | tf_op jit(solution)/shard_map/slice | solution.py:75
Sparse Core Ops, SparseCore 0:
  28.7 56.5 all-gather.1
where the time goes:
time: 101 us
  waiting for transfers between devices  29 us (29%)
  between operations  26.1 us (26%)
  local copies, waits for them, and re-layouts  18.8 us (19%)
  starting transfers between devices  13.3 us (13%)
  matrix products  7.73 us (8%)
  other arithmetic  5.89 us (6%)
    all_gather x1, waiting for transfers between devices, on_device(): all_states = lax.all_gather(state, 'inst', axis=0, tiled=True)  28.9 us
    ppermute x4, starting transfers between devices, passed_along(): return lax.ppermute(value, axis, pairs)  13.3 us
    dot_general x1, matrix products, on_device(): jnp.einsum('nm,mvbij->nvbij', own_rows, all_states, precision=lax.Precisi...  7.73 us
    slice x2, local copies, waits for them, and re-layouts, spatial_residual(): jnp.roll(fields, 1, 4)  2.62 us
    slice x2, local copies, waits for them, and re-layouts, spatial_residual(): jnp.roll(fields, 2, 4)  2.58 us
    slice x2, local copies, waits for them, and re-layouts, spatial_residual(): jnp.roll(flux_cols, 1, 4)  2.56 us
    unnamed x7, other arithmetic  2.49 us
  transfers between devices with their start and end apart: 5, of which 1 were waited for; matrix products, arithmetic and copies ran while one was open for 18% of the time, Pallas kernels for 0%

commit v1 on v0

v1 whole, which is shorter than its diff:
```python
import functools
import math

import jax
import jax.numpy as jnp
from jax import lax
from jax.experimental import pallas as pl
from jax.experimental.pallas import tpu as pltpu
from jax.sharding import PartitionSpec as P

REACH = 2
GAMMA_MINUS = 0.4
DAMPING = 0.05
FREQUENCY = 1.0
MESH = pl.DeviceIdType.MESH
STEPS = [step for step in range(-REACH, REACH + 1) if step != 0]
EARLY = 2


def spectral_weight(offset, count):
    offset %= count
    if offset == 0 or 2 * offset == count:
        return 0.0
    return 0.5 * FREQUENCY * (-1.0) ** offset / math.tan(math.pi * offset / count)


def weighted_sum(weights, values):
    total = None
    for weight, value in zip(weights, values):
        if weight == 0.0:
            continue
        term = weight * value
        total = term if total is None else total + term
    return total


def differences(flux, fields, axis):
    size = fields.shape[axis]
    wide = flux * (8.0 / 12.0)
    narrow = flux * (1.0 / 12.0)
    near = fields * (4.0 * DAMPING)
    far = fields * DAMPING
    ahead = (near - wide) + pltpu.roll(narrow - far, size - 1, axis)
    behind = (near + wide) - pltpu.roll(narrow + far, 1, axis)
    return (
        pltpu.roll(ahead, size - 1, axis)
        + pltpu.roll(behind, 1, axis)
        - fields * (6.0 * DAMPING)
    )


def flux_parts(fields, pressure, inverse, direction):
    velocity = fields[direction] * inverse
    parts = [
        fields[direction],
        fields[1] * velocity,
        fields[2] * velocity,
        fields[3] * velocity,
        (fields[4] + pressure) * velocity,
    ]
    parts[direction] = parts[direction] + pressure
    return parts


def kernel(
    instances, x_hbm, slot_hbm, block_hbm, side_hbm, shift_hbm, rows_hbm, out,
    near, far, rims, ghosts, slot, block, side, shift, rows,
    in_sems, far_send, far_recv, rim_send, rim_recv,
):
    here, count_v, row_count, columns = near.shape
    inst = lax.axis_index("inst")
    me = lax.axis_index("blk")
    span = lax.axis_size("blk")
    partner = (1 - inst, me)

    local = [
        pltpu.make_async_copy(source, target, in_sems.at[place])
        for place, (source, target) in enumerate(
            [
                (slot_hbm, slot),
                (rows_hbm, rows),
                (block_hbm, block),
                (side_hbm, side),
                (shift_hbm, shift),
                (x_hbm, near),
            ]
        )
    ]
    for copy in local:
        copy.start()

    barrier = pltpu.get_barrier_semaphore()
    pl.semaphore_signal(barrier, inc=1, device_id=partner, device_id_type=MESH)
    for step in STEPS:
        pl.semaphore_signal(
            barrier,
            inc=1,
            device_id=(inst, lax.rem(me + step + span, span)),
            device_id_type=MESH,
        )
    pl.semaphore_wait(barrier, 1 + len(STEPS))

    far_copies = [
        pltpu.make_async_remote_copy(
            src_ref=x_hbm.at[:, v],
            dst_ref=far.at[:, v],
            send_sem=far_send.at[v],
            recv_sem=far_recv.at[v],
            device_id=partner,
            device_id_type=MESH,
        )
        for v in range(count_v)
    ]
    for copy in far_copies[:EARLY]:
        copy.start()

    for copy in local:
        copy.wait()
    slots = slot[...]
    numbers = lax.broadcasted_iota(jnp.int32, slots.shape, 1)
    mine = slots == me

    def looked_up(mask, values):
        return jnp.sum(jnp.where(mask, values, 0))

    my_rows = looked_up(mine, rows[...])
    picks = []
    shifts = []
    for face in range(2):
        neighbour = looked_up(mine, block[face : face + 1, :])
        neighbour_slot = looked_up(numbers == neighbour, slots)
        distance = lax.rem(neighbour_slot - me + (REACH + span), span)
        picks.append(
            jnp.clip(
                2 * distance + looked_up(mine, side[face : face + 1, :]), 0, rims.shape[0] - 1
            )
        )
        shifts.append(looked_up(mine, shift[face : face + 1, :]))

    high = [jnp.clip(my_rows - 1 - layer, 0, row_count - 1) for layer in range(2)]

    def gather_rim(v, carry):
        for n in range(here):
            rims[2 * REACH, v, 2 * n : 2 * n + 2, :] = near[n, v, 0:2, :]
            for layer in range(2):
                rims[2 * REACH + 1, v, 2 * n + layer : 2 * n + layer + 1, :] = near[
                    n, v, pl.ds(high[layer], 1), :
                ]
        return carry

    lax.fori_loop(0, count_v, gather_rim, 0)

    rim_copies = [
        pltpu.make_async_remote_copy(
            src_ref=rims.at[2 * REACH : 2 * REACH + 2],
            dst_ref=rims.at[2 * (REACH - step) : 2 * (REACH - step) + 2],
            send_sem=rim_send.at[REACH - step],
            recv_sem=rim_recv.at[REACH - step],
            device_id=(inst, lax.rem(me + step + span, span)),
            device_id_type=MESH,
        )
        for step in STEPS
    ]
    for copy in rim_copies:
        copy.start()
    for copy in far_copies[EARLY:]:
        copy.start()

    def own_source(v, carry):
        values = [near[m, v] for m in range(here)]
        for n in range(here):
            out[n, v] = weighted_sum(
                [-spectral_weight(n - m, instances) for m in range(here)], values
            )
        return carry

    lax.fori_loop(0, count_v, own_source, 0)

    for copy in rim_copies:
        copy.wait_recv()
    for face in range(2):
        picked = rims[picks[face]]
        amount = columns - shifts[face]
        for v in range(count_v):
            ghosts[face, v] = pltpu.roll(picked[v], amount, 1)

    extent = row_count + 8
    position = lax.broadcasted_iota(jnp.int32, (extent, columns), 0)
    first_beyond = position == my_rows
    second_beyond = position == my_rows + 1
    last_row = lax.broadcasted_iota(jnp.int32, (8, columns), 0) == 7

    def spatial(n, carry):
        fields = []
        for v in range(count_v):
            low = [ghosts[0, v, pl.ds(2 * n + layer, 1), :] for layer in range(2)]
            top = [ghosts[1, v, pl.ds(2 * n + layer, 1), :] for layer in range(2)]
            before = jnp.where(last_row, low[0], low[1])
            block_rows = jnp.concatenate([near[n, v], before], axis=0)
            fields.append(
                jnp.where(first_beyond, top[0], jnp.where(second_beyond, top[1], block_rows))
            )
        inverse = 1.0 / fields[0]
        squares = fields[1] * fields[1] + fields[2] * fields[2] + fields[3] * fields[3]
        pressure = GAMMA_MINUS * (fields[4] - 0.5 * squares * inverse)
        for v, flux in enumerate(flux_parts(fields, pressure, inverse, 1)):
            out[n, v] += differences(flux, fields[v], 0)[:row_count]
        fields = [field[:row_count] for field in fields]
        pressure = pressure[:row_count]
        inverse = inverse[:row_count]
        for v, flux in enumerate(flux_parts(fields, pressure, inverse, 2)):
            out[n, v] += differences(flux, fields[v], 1)
        return carry

    lax.fori_loop(0, here, spatial, 0)

    inside = lax.broadcasted_iota(jnp.int32, (row_count, columns), 0) < my_rows
    for v in range(count_v):
        far_copies[v].wait_recv()
        values = [far[m, v] for m in range(here)]
        for n in range(here):
            source = weighted_sum(
                [spectral_weight(n - m - here, instances) for m in range(here)], values
            )
            out[n, v] = jnp.where(inside, out[n, v] - source, 0.0)
    for copy in far_copies + rim_copies:
        copy.wait_send()


def on_device(state, slot_of, conn_block, conn_side, conn_shift, rows):
    here, count_v, _, row_count, columns = state.shape
    instances = here * lax.axis_size("inst")
    blocks = slot_of.shape[0]
    whole = (here, count_v, row_count, columns)
    result = pl.pallas_call(
        functools.partial(kernel, instances),
        out_shape=jax.ShapeDtypeStruct(whole, jnp.float32),
        in_specs=[pl.BlockSpec(memory_space=pl.ANY)] * 6,
        out_specs=pl.BlockSpec(memory_space=pltpu.VMEM),
        scratch_shapes=[
            pltpu.VMEM(whole, jnp.float32),
            pltpu.VMEM(whole, jnp.float32),
            pltpu.VMEM((2 * (2 * REACH + 1), count_v, 2 * here, columns), jnp.float32),
            pltpu.VMEM((2, count_v, 2 * here, columns), jnp.float32),
            pltpu.VMEM((1, blocks), jnp.int32),
            pltpu.VMEM((2, blocks), jnp.int32),
            pltpu.VMEM((2, blocks), jnp.int32),
            pltpu.VMEM((2, blocks), jnp.int32),
            pltpu.VMEM((1, blocks), jnp.int32),
            pltpu.SemaphoreType.DMA((6,)),
            pltpu.SemaphoreType.DMA((count_v,)),
            pltpu.SemaphoreType.DMA((count_v,)),
            pltpu.SemaphoreType.DMA((2 * REACH + 1,)),
            pltpu.SemaphoreType.DMA((2 * REACH + 1,)),
        ],
        compiler_params=pltpu.CompilerParams(collective_id=0, has_side_effects=True),
        name="residual",
    )(
        state.reshape(whole),
        slot_of.reshape(1, blocks),
        conn_block.T,
        conn_side.T,
        conn_shift.T,
        rows.reshape(1, blocks),
    )
    return result.reshape(state.shape)


def solution(mesh):
    in_specs = (P("inst", None, "blk", None, None), P(), P(), P(), P(), P())
    out_specs = P("inst", None, "blk", None, None)
    return jax.shard_map(
        on_device, mesh=mesh, in_specs=in_specs, out_specs=out_specs, check_vma=False
    )
```

time: 101 us -> 45.1 us (0.45)
  the two profiles are of different devices: /device:TPU:9 before, /device:TPU:1 now
where the time goes in v1:
time: 45.1 us; the launch traced here: 44.9 us
  Pallas kernels  42.9 us (95%)
  local copies, waits for them, and re-layouts  1.99 us (4%)
    pallas_call x1, Pallas kernels, on_device(): pl.pallas_call(functools.partial(kernel, instances), out_shape=jax.ShapeD...  42.9 us
    unnamed x1, local copies, waits for them, and re-layouts  1.99 us

profile of v1, /device:TPU:1, one launch (start us, length us, event | category | flops | bytes accessed | tf_op | source)
XLA Modules:
  0.0 44.9 jit_solution(13343418171578260930)
XLA Ops:
  0.0 42.9 %residual.1 = f32[4,5,32,256]{3,2,1,0:T(8,128)} custom-call(f32[4,5,32,256]{3,2,1,0:T(8,128)} %bitcast.10, s32[1,256]{1,0:T(1,128)} %bitcast.14, s32[2,256]{1,0:T(2,128)} %bitcast.11, s32[2,256]{1,0:T(2,128)} %bitcast.12, s32[2,256]{1,0:T(2,128)} %bitcast.13, s32[1,256]{1,0:T(1,128)} %bitcast.15), custom_call_target="tpu_custom_call" | custom-call | tf_op jit(solution)/shard_map/residual/pallas_call | solution.py:235
  42.9 2.0 %copy.9 = f32[4,5,1,32,256]{4,3,2,1,0:T(8,128)} copy(f32[4,5,1,32,256]{4,3,2,1,0:T(8,128)} %bitcast.9) | data formatting | bytes 1310720

commit v2 on v1

--- a/solution.py
+++ b/solution.py
@@ -13,8 +13,9 @@
 DAMPING = 0.05
 FREQUENCY = 1.0
 MESH = pl.DeviceIdType.MESH
-STEPS = [step for step in range(-REACH, REACH + 1) if step != 0]
-EARLY = 2
+OWN = REACH
+STEPS = (-2, 2, -1, 1)
+BATCHES = (4, 12)
 
 
 def spectral_weight(offset, count):
@@ -65,17 +66,30 @@
 def kernel(
     instances, x_hbm, slot_hbm, block_hbm, side_hbm, shift_hbm, rows_hbm, out,
     near, far, rims, ghosts, slot, block, side, shift, rows,
-    in_sems, far_send, far_recv, rim_send, rim_recv,
+    in_sems, far_send, far_recv, rim_send, rim_recv, hop, hop_sems,
 ):
     here, count_v, row_count, columns = near.shape
     inst = lax.axis_index("inst")
     me = lax.axis_index("blk")
     span = lax.axis_size("blk")
     partner = (1 - inst, me)
+    place = lax.rem(me // 2, 4)
+
+    def at(step):
+        return (inst, lax.rem(me + step + span, span))
+
+    ends = (place == 0) | (place == 3)
+    aside = 2 - 4 * lax.rem(place, 2)
+    beside = lax.rem(me + aside + span, span)
+
+    barrier = pltpu.get_barrier_semaphore()
+    peers = [partner, (1 - inst, beside)] + [at(step) for step in STEPS]
+    for device in peers:
+        pl.semaphore_signal(barrier, inc=1, device_id=device, device_id_type=MESH)
 
     local = [
-        pltpu.make_async_copy(source, target, in_sems.at[place])
-        for place, (source, target) in enumerate(
+        pltpu.make_async_copy(source, target, in_sems.at[index])
+        for index, (source, target) in enumerate(
             [
                 (slot_hbm, slot),
                 (rows_hbm, rows),
@@ -89,30 +103,44 @@
     for copy in local:
         copy.start()
 
-    barrier = pltpu.get_barrier_semaphore()
-    pl.semaphore_signal(barrier, inc=1, device_id=partner, device_id_type=MESH)
-    for step in STEPS:
-        pl.semaphore_signal(
-            barrier,
-            inc=1,
-            device_id=(inst, lax.rem(me + step + span, span)),
-            device_id_type=MESH,
-        )
-    pl.semaphore_wait(barrier, 1 + len(STEPS))
+    pl.semaphore_wait(barrier, len(peers))
 
     far_copies = [
         pltpu.make_async_remote_copy(
-            src_ref=x_hbm.at[:, v],
-            dst_ref=far.at[:, v],
-            send_sem=far_send.at[v],
-            recv_sem=far_recv.at[v],
+            src_ref=x_hbm.at[m, v],
+            dst_ref=far.at[m, v],
+            send_sem=far_send.at[m, v],
+            recv_sem=far_recv.at[m, v],
             device_id=partner,
             device_id_type=MESH,
         )
         for v in range(count_v)
+        for m in range(here)
     ]
-    for copy in far_copies[:EARLY]:
-        copy.start()
+    moved = far_copies.pop()
+    aside_copy = pltpu.make_async_remote_copy(
+        src_ref=x_hbm.at[here - 1, count_v - 1],
+        dst_ref=hop,
+        send_sem=hop_sems.at[0],
+        recv_sem=hop_sems.at[1],
+        device_id=(inst, beside),
+        device_id_type=MESH,
+    )
+    onward_copy = pltpu.make_async_remote_copy(
+        src_ref=hop,
+        dst_ref=far.at[here - 1, count_v - 1],
+        send_sem=hop_sems.at[2],
+        recv_sem=far_recv.at[here - 1, count_v - 1],
+        device_id=(1 - inst, beside),
+        device_id_type=MESH,
+    )
+    started = [0, BATCHES[0], sum(BATCHES), len(far_copies)]
+
+    def start_far(batch):
+        for copy in far_copies[started[batch] : started[batch + 1]]:
+            copy.start()
+
+    start_far(0)
 
     for copy in local:
         copy.wait()
@@ -141,9 +169,9 @@
 
     def gather_rim(v, carry):
         for n in range(here):
-            rims[2 * REACH, v, 2 * n : 2 * n + 2, :] = near[n, v, 0:2, :]
+            rims[2 * OWN, v, 2 * n : 2 * n + 2, :] = near[n, v, 0:2, :]
             for layer in range(2):
-                rims[2 * REACH + 1, v, 2 * n + layer : 2 * n + layer + 1, :] = near[
+                rims[2 * OWN + 1, v, 2 * n + layer : 2 * n + layer + 1, :] = near[
                     n, v, pl.ds(high[layer], 1), :
                 ]
         return carry
@@ -152,19 +180,19 @@
 
     rim_copies = [
         pltpu.make_async_remote_copy(
-            src_ref=rims.at[2 * REACH : 2 * REACH + 2],
-            dst_ref=rims.at[2 * (REACH - step) : 2 * (REACH - step) + 2],
-            send_sem=rim_send.at[REACH - step],
-            recv_sem=rim_recv.at[REACH - step],
-            device_id=(inst, lax.rem(me + step + span, span)),
+            src_ref=rims.at[2 * OWN : 2 * OWN + 2],
+            dst_ref=rims.at[2 * (OWN - step) : 2 * (OWN - step) + 2],
+            send_sem=rim_send.at[OWN - step],
+            recv_sem=rim_recv.at[OWN - step],
+            device_id=at(step),
             device_id_type=MESH,
         )
         for step in STEPS
     ]
     for copy in rim_copies:
         copy.start()
-    for copy in far_copies[EARLY:]:
-        copy.start()
+    pl.when(ends)(aside_copy.start)
+    start_far(1)
 
     def own_source(v, carry):
         values = [near[m, v] for m in range(here)]
@@ -176,6 +204,13 @@
 
     lax.fori_loop(0, count_v, own_source, 0)
 
+    @pl.when(jnp.logical_not(ends))
+    def _():
+        aside_copy.wait_recv()
+        onward_copy.start()
+        moved.start()
+
+    start_far(2)
     for copy in rim_copies:
         copy.wait_recv()
     for face in range(2):
@@ -216,7 +251,8 @@
 
     inside = lax.broadcasted_iota(jnp.int32, (row_count, columns), 0) < my_rows
     for v in range(count_v):
-        far_copies[v].wait_recv()
+        for copy in (far_copies + [moved])[v * here : (v + 1) * here]:
+            copy.wait_recv()
         values = [far[m, v] for m in range(here)]
         for n in range(here):
             source = weighted_sum(
@@ -225,6 +261,12 @@
             out[n, v] = jnp.where(inside, out[n, v] - source, 0.0)
     for copy in far_copies + rim_copies:
         copy.wait_send()
+    pl.when(ends)(aside_copy.wait_send)
+
+    @pl.when(jnp.logical_not(ends))
+    def _():
+        onward_copy.wait_send()
+        moved.wait_send()
 
 
 def on_device(state, slot_of, conn_block, conn_side, conn_shift, rows):
@@ -248,20 +290,29 @@
             pltpu.VMEM((2, blocks), jnp.int32),
             pltpu.VMEM((1, blocks), jnp.int32),
             pltpu.SemaphoreType.DMA((6,)),
-            pltpu.SemaphoreType.DMA((count_v,)),
-            pltpu.SemaphoreType.DMA((count_v,)),
+            pltpu.SemaphoreType.DMA((here, count_v)),
+            pltpu.SemaphoreType.DMA((here, count_v)),
             pltpu.SemaphoreType.DMA((2 * REACH + 1,)),
             pltpu.SemaphoreType.DMA((2 * REACH + 1,)),
+            pltpu.VMEM((row_count, columns), jnp.float32),
+            pltpu.SemaphoreType.DMA((3,)),
         ],
-        compiler_params=pltpu.CompilerParams(collective_id=0, has_side_effects=True),
+        compiler_params=pltpu.CompilerParams(
+            collective_id=0, has_side_effects=True, vmem_limit_bytes=16 * 2**20
+        ),
         name="residual",
     )(
-        state.reshape(whole),
-        slot_of.reshape(1, blocks),
-        conn_block.T,
-        conn_side.T,
-        conn_shift.T,
-        rows.reshape(1, blocks),
+        *[
+            pltpu.with_memory_space_constraint(operand, pltpu.HBM)
+            for operand in (
+                state.reshape(whole),
+                slot_of.reshape(1, blocks),
+                conn_block.T,
+                conn_side.T,
+                conn_shift.T,
+                rows.reshape(1, blocks),
+            )
+        ]
     )
     return result.reshape(state.shape)
 

time: 45.1 us -> 42.9 us (0.951)
  local copies, waits for them, and re-layouts: 1.99 us -> 0.84 us
  Pallas kernels: 42.9 us -> 41.9 us
    unnamed x1, local copies, waits for them, and re-layouts: 1.99 us -> 0.84 us
    pallas_call x1, Pallas kernels: 42.9 us -> 41.9 us  [on_device(): pl.pallas_call(functools.partial(kernel, instances), out_shape=jax.ShapeD...]
where the time goes in v2:
time: 42.9 us; the launch traced here: 42.8 us
  Pallas kernels  41.9 us (98%)
  local copies, waits for them, and re-layouts  0.84 us (2%)
    pallas_call x1, Pallas kernels, on_device(): pl.pallas_call(functools.partial(kernel, instances), out_shape=jax.ShapeD...  41.9 us

profile of v2, /device:TPU:1, one launch (start us, length us, event | category | flops | bytes accessed | tf_op | source)
XLA Modules:
  0.0 42.8 jit_solution(6018126029462523340)
XLA Ops:
  0.0 41.9 %residual.1 = f32[4,5,32,256]{3,2,1,0:T(8,128)S(1)} custom-call(f32[4,5,32,256]{3,2,1,0:T(8,128)} %bitcast.10, s32[1,256]{1,0:T(1,128)} %bitcast.14, s32[2,256]{1,0:T(2,128)} %bitcast.11, s32[2,256]{1,0:T(2,128)} %bitcast.12, s32[2,256]{1,0:T(2,128)} %bitcast.13, s32[1,256]{1,0:T(1,128)} %bitcast.15), custom_call_target="tpu_custom_call" | custom-call | tf_op jit(solution)/shard_map/residual/pallas_call | solution.py:277
  41.9 0.8 %copy.9 = f32[4,5,1,32,256]{4,3,2,1,0:T(8,128)} copy(f32[4,5,1,32,256]{4,3,2,1,0:T(8,128)S(1)} %bitcast.9) | data formatting | bytes 1310720

commit v3 on v2

--- a/solution.py
+++ b/solution.py
@@ -66,7 +66,7 @@
 def kernel(
     instances, x_hbm, slot_hbm, block_hbm, side_hbm, shift_hbm, rows_hbm, out,
     near, far, rims, ghosts, slot, block, side, shift, rows,
-    in_sems, far_send, far_recv, rim_send, rim_recv, hop, hop_sems,
+    in_sems, far_send, far_recv, rim_send, rim_recv, hop, hop_sems, ack, cross,
 ):
     here, count_v, row_count, columns = near.shape
     inst = lax.axis_index("inst")
@@ -82,10 +82,19 @@
     aside = 2 - 4 * lax.rem(place, 2)
     beside = lax.rem(me + aside + span, span)
 
+    def signal(semaphore, device):
+        pl.semaphore_signal(semaphore, inc=1, device_id=device, device_id_type=MESH)
+
+    below = {step: lax.rem(me + step + span, span) < me for step in STEPS}
+    above = {step: lax.rem(me + step + span, span) > me for step in STEPS}
     barrier = pltpu.get_barrier_semaphore()
-    peers = [partner, (1 - inst, beside)] + [at(step) for step in STEPS]
-    for device in peers:
-        pl.semaphore_signal(barrier, inc=1, device_id=device, device_id_type=MESH)
+    signal(barrier, partner)
+    for step in STEPS:
+        pl.when(above[step])(functools.partial(signal, barrier, at(step)))
+    pl.when(inst == 0)(functools.partial(signal, barrier, (1 - inst, beside)))
+    greetings = 1 + inst
+    for step in STEPS:
+        greetings = greetings + jnp.where(below[step], 1, 0)
 
     local = [
         pltpu.make_async_copy(source, target, in_sems.at[index])
@@ -103,7 +112,7 @@
     for copy in local:
         copy.start()
 
-    pl.semaphore_wait(barrier, len(peers))
+    pl.semaphore_wait(barrier, greetings)
 
     far_copies = [
         pltpu.make_async_remote_copy(
@@ -141,6 +150,9 @@
             copy.start()
 
     start_far(0)
+    for step in STEPS:
+        pl.when(below[step])(functools.partial(signal, ack.at[STEPS.index(-step)], at(step)))
+    pl.when((inst == 1) & ends)(functools.partial(signal, cross, (1 - inst, beside)))
 
     for copy in local:
         copy.wait()
@@ -189,8 +201,14 @@
         )
         for step in STEPS
     ]
-    for copy in rim_copies:
-        copy.start()
+    def answered(step):
+        pl.semaphore_wait(ack.at[STEPS.index(step)], 1)
+        rim_copies[STEPS.index(step)].start()
+
+    for step, copy in zip(STEPS, rim_copies):
+        pl.when(below[step])(copy.start)
+    for step in (1, 2):
+        pl.when(above[step])(functools.partial(answered, step))
     pl.when(ends)(aside_copy.start)
     start_far(1)
 
@@ -204,13 +222,18 @@
 
     lax.fori_loop(0, count_v, own_source, 0)
 
-    @pl.when(jnp.logical_not(ends))
+    middle = jnp.logical_not(ends)
+    pl.when(middle & (inst == 0))(functools.partial(pl.semaphore_wait, cross, 1))
+
+    @pl.when(middle)
     def _():
         aside_copy.wait_recv()
         onward_copy.start()
         moved.start()
 
     start_far(2)
+    for step in (-1, -2):
+        pl.when(above[step])(functools.partial(answered, step))
     for copy in rim_copies:
         copy.wait_recv()
     for face in range(2):
@@ -296,6 +319,8 @@
             pltpu.SemaphoreType.DMA((2 * REACH + 1,)),
             pltpu.VMEM((row_count, columns), jnp.float32),
             pltpu.SemaphoreType.DMA((3,)),
+            pltpu.SemaphoreType.REGULAR((4,)),
+            pltpu.SemaphoreType.REGULAR,
         ],
         compiler_params=pltpu.CompilerParams(
             collective_id=0, has_side_effects=True, vmem_limit_bytes=16 * 2**20

time: 42.9 us -> 41.4 us (0.965)
  the two profiles are of different devices: /device:TPU:1 before, /device:TPU:448 now
where the time goes in v3:
time: 41.4 us; the launch traced here: 41.2 us
  Pallas kernels  40.4 us (98%)
  local copies, waits for them, and re-layouts  0.84 us (2%)
    pallas_call x1, Pallas kernels, on_device(): pl.pallas_call(functools.partial(kernel, instances), out_shape=jax.ShapeD...  40.4 us
    unnamed x1, local copies, waits for them, and re-layouts  0.84 us

profile of v3, /device:TPU:448, one launch (start us, length us, event | category | flops | bytes accessed | tf_op | source)
XLA Modules:
  0.0 41.2 jit_solution(8008079546878103465)
XLA Ops:
  0.0 40.4 %residual.1 = f32[4,5,32,256]{3,2,1,0:T(8,128)S(1)} custom-call(f32[4,5,32,256]{3,2,1,0:T(8,128)} %bitcast.10, s32[1,256]{1,0:T(1,128)} %bitcast.14, s32[2,256]{1,0:T(2,128)} %bitcast.11, s32[2,256]{1,0:T(2,128)} %bitcast.12, s32[2,256]{1,0:T(2,128)} %bitcast.13, s32[1,256]{1,0:T(1,128)} %bitcast.15), custom_call_target="tpu_custom_call" | custom-call | tf_op jit(solution)/shard_map/residual/pallas_call | solution.py:300
  40.4 0.8 %copy.9 = f32[4,5,1,32,256]{4,3,2,1,0:T(8,128)} copy(f32[4,5,1,32,256]{4,3,2,1,0:T(8,128)S(1)} %bitcast.9) | data formatting | bytes 1310720

commit v4 on v3

--- a/solution.py
+++ b/solution.py
@@ -15,7 +15,9 @@
 MESH = pl.DeviceIdType.MESH
 OWN = REACH
 STEPS = (-2, 2, -1, 1)
-BATCHES = (4, 12)
+EARLY = 6
+HELD = 3
+ASIDE = 2
 
 
 def spectral_weight(offset, count):
@@ -126,30 +128,37 @@
         for v in range(count_v)
         for m in range(here)
     ]
-    moved = far_copies.pop()
-    aside_copy = pltpu.make_async_remote_copy(
-        src_ref=x_hbm.at[here - 1, count_v - 1],
-        dst_ref=hop,
-        send_sem=hop_sems.at[0],
-        recv_sem=hop_sems.at[1],
-        device_id=(inst, beside),
-        device_id_type=MESH,
-    )
-    onward_copy = pltpu.make_async_remote_copy(
-        src_ref=hop,
-        dst_ref=far.at[here - 1, count_v - 1],
-        send_sem=hop_sems.at[2],
-        recv_sem=far_recv.at[here - 1, count_v - 1],
-        device_id=(1 - inst, beside),
-        device_id_type=MESH,
-    )
-    started = [0, BATCHES[0], sum(BATCHES), len(far_copies)]
-
-    def start_far(batch):
-        for copy in far_copies[started[batch] : started[batch + 1]]:
-            copy.start()
-
-    start_far(0)
+    middle = jnp.logical_not(ends)
+    sends = [ends, place == 0]
+    passes = [middle, place == 1]
+    always = far_copies[: len(far_copies) - ASIDE]
+    moved = far_copies[: len(always) - 1 : -1]
+    aside_copies = []
+    onward_copies = []
+    for piece in range(ASIDE):
+        v, m = divmod(len(far_copies) - 1 - piece, here)
+        aside_copies.append(
+            pltpu.make_async_remote_copy(
+                src_ref=x_hbm.at[m, v],
+                dst_ref=hop.at[piece],
+                send_sem=hop_sems.at[0, piece],
+                recv_sem=hop_sems.at[1, piece],
+                device_id=(inst, beside),
+                device_id_type=MESH,
+            )
+        )
+        onward_copies.append(
+            pltpu.make_async_remote_copy(
+                src_ref=hop.at[piece],
+                dst_ref=far.at[m, v],
+                send_sem=hop_sems.at[2, piece],
+                recv_sem=far_recv.at[m, v],
+                device_id=(1 - inst, beside),
+                device_id_type=MESH,
+            )
+        )
+    for copy in always[:EARLY]:
+        copy.start()
     for step in STEPS:
         pl.when(below[step])(functools.partial(signal, ack.at[STEPS.index(-step)], at(step)))
     pl.when((inst == 1) & ends)(functools.partial(signal, cross, (1 - inst, beside)))
@@ -209,8 +218,10 @@
         pl.when(below[step])(copy.start)
     for step in (1, 2):
         pl.when(above[step])(functools.partial(answered, step))
-    pl.when(ends)(aside_copy.start)
-    start_far(1)
+    for piece in range(ASIDE):
+        pl.when(sends[piece])(aside_copies[piece].start)
+    for copy in always[EARLY : len(always) - HELD]:
+        copy.start()
 
     def own_source(v, carry):
         values = [near[m, v] for m in range(here)]
@@ -222,16 +233,18 @@
 
     lax.fori_loop(0, count_v, own_source, 0)
 
-    middle = jnp.logical_not(ends)
     pl.when(middle & (inst == 0))(functools.partial(pl.semaphore_wait, cross, 1))
 
-    @pl.when(middle)
-    def _():
-        aside_copy.wait_recv()
-        onward_copy.start()
-        moved.start()
-
-    start_far(2)
+    def pass_on(piece):
+        aside_copies[piece].wait_recv()
+        onward_copies[piece].start()
+
+    for piece in range(ASIDE):
+        pl.when(passes[piece])(functools.partial(pass_on, piece))
+    for copy in always[len(always) - HELD :]:
+        copy.start()
+    for piece in range(ASIDE):
+        pl.when(jnp.logical_not(sends[piece]))(moved[piece].start)
     for step in (-1, -2):
         pl.when(above[step])(functools.partial(answered, step))
     for copy in rim_copies:
@@ -274,7 +287,7 @@
 
     inside = lax.broadcasted_iota(jnp.int32, (row_count, columns), 0) < my_rows
     for v in range(count_v):
-        for copy in (far_copies + [moved])[v * here : (v + 1) * here]:
+        for copy in far_copies[v * here : (v + 1) * here]:
             copy.wait_recv()
         values = [far[m, v] for m in range(here)]
         for n in range(here):
@@ -282,14 +295,12 @@
                 [spectral_weight(n - m - here, instances) for m in range(here)], values
             )
             out[n, v] = jnp.where(inside, out[n, v] - source, 0.0)
-    for copy in far_copies + rim_copies:
+    for copy in always + rim_copies:
         copy.wait_send()
-    pl.when(ends)(aside_copy.wait_send)
-
-    @pl.when(jnp.logical_not(ends))
-    def _():
-        onward_copy.wait_send()
-        moved.wait_send()
+    for piece in range(ASIDE):
+        pl.when(sends[piece])(aside_copies[piece].wait_send)
+        pl.when(passes[piece])(onward_copies[piece].wait_send)
+        pl.when(jnp.logical_not(sends[piece]))(moved[piece].wait_send)
 
 
 def on_device(state, slot_of, conn_block, conn_side, conn_shift, rows):
@@ -317,8 +328,8 @@
             pltpu.SemaphoreType.DMA((here, count_v)),
             pltpu.SemaphoreType.DMA((2 * REACH + 1,)),
             pltpu.SemaphoreType.DMA((2 * REACH + 1,)),
-            pltpu.VMEM((row_count, columns), jnp.float32),
-            pltpu.SemaphoreType.DMA((3,)),
+            pltpu.VMEM((ASIDE, row_count, columns), jnp.float32),
+            pltpu.SemaphoreType.DMA((3, ASIDE)),
             pltpu.SemaphoreType.REGULAR((4,)),
             pltpu.SemaphoreType.REGULAR,
         ],

time: 41.4 us -> 40.2 us (0.971)
  the two profiles are of different devices: /device:TPU:448 before, /device:TPU:466 now
where the time goes in v4:
time: 40.2 us; the launch traced here: 40 us
  Pallas kernels  39.2 us (98%)
  local copies, waits for them, and re-layouts  0.84 us (2%)
    pallas_call x1, Pallas kernels, on_device(): pl.pallas_call(functools.partial(kernel, instances), out_shape=jax.ShapeD...  39.2 us
    unnamed x1, local copies, waits for them, and re-layouts  0.84 us

profile of v4, /device:TPU:466, one launch (start us, length us, event | category | flops | bytes accessed | tf_op | source)
XLA Modules:
  0.0 40.0 jit_solution(6281233148881268682)
XLA Ops:
  0.0 39.2 %residual.1 = f32[4,5,32,256]{3,2,1,0:T(8,128)S(1)} custom-call(f32[4,5,32,256]{3,2,1,0:T(8,128)} %bitcast.10, s32[1,256]{1,0:T(1,128)} %bitcast.14, s32[2,256]{1,0:T(2,128)} %bitcast.11, s32[2,256]{1,0:T(2,128)} %bitcast.12, s32[2,256]{1,0:T(2,128)} %bitcast.13, s32[1,256]{1,0:T(1,128)} %bitcast.15), custom_call_target="tpu_custom_call" | custom-call | tf_op jit(solution)/shard_map/residual/pallas_call | solution.py:311
  39.2 0.8 %copy.9 = f32[4,5,1,32,256]{4,3,2,1,0:T(8,128)} copy(f32[4,5,1,32,256]{4,3,2,1,0:T(8,128)S(1)} %bitcast.9) | data formatting | bytes 1310720

commit v5 on v4

--- a/solution.py
+++ b/solution.py
@@ -18,6 +18,7 @@
 EARLY = 6
 HELD = 3
 ASIDE = 2
+FIRST_ROW = 8
 
 
 def spectral_weight(offset, count):
@@ -68,7 +69,7 @@
 def kernel(
     instances, x_hbm, slot_hbm, block_hbm, side_hbm, shift_hbm, rows_hbm, out,
     near, far, rims, ghosts, slot, block, side, shift, rows,
-    in_sems, far_send, far_recv, rim_send, rim_recv, hop, hop_sems, ack, cross,
+    in_sems, far_send, far_recv, rim_send, rim_recv, hop, hop_sems, ack, cross, helper, share_sem,
 ):
     here, count_v, row_count, columns = near.shape
     inst = lax.axis_index("inst")
@@ -80,21 +81,34 @@
     def at(step):
         return (inst, lax.rem(me + step + span, span))
 
-    ends = (place == 0) | (place == 3)
-    aside = 2 - 4 * lax.rem(place, 2)
-    beside = lax.rem(me + aside + span, span)
+    rest = me >= FIRST_ROW
+    first = rest & (place == 0)
+    helps = [rest & (place == piece + 1) for piece in range(ASIDE)]
+    beside = [
+        lax.rem(me + (2 + 2 * piece) * jnp.where(place == 0, 1, -1) + span, span)
+        for piece in range(ASIDE)
+    ]
 
     def signal(semaphore, device):
         pl.semaphore_signal(semaphore, inc=1, device_id=device, device_id_type=MESH)
 
-    below = {step: lax.rem(me + step + span, span) < me for step in STEPS}
-    above = {step: lax.rem(me + step + span, span) > me for step in STEPS}
+    def order(index):
+        return jnp.where(index == 0, 5, 2 * index)
+
+    below = {step: order(lax.rem(me + step + span, span)) < order(me) for step in STEPS}
+    above = {step: jnp.logical_not(below[step]) for step in STEPS}
     barrier = pltpu.get_barrier_semaphore()
     signal(barrier, partner)
     for step in STEPS:
         pl.when(above[step])(functools.partial(signal, barrier, at(step)))
-    pl.when(inst == 0)(functools.partial(signal, barrier, (1 - inst, beside)))
-    greetings = 1 + inst
+    greetings = 1 + jnp.where(helps[1], 1, 0)
+    pl.when(first)(functools.partial(signal, barrier, (inst, beside[1])))
+    for piece in range(ASIDE):
+        takes_part = first | helps[piece]
+        greetings = greetings + inst * jnp.where(takes_part, 1, 0)
+        pl.when((inst == 0) & takes_part)(
+            functools.partial(signal, barrier, (1 - inst, beside[piece]))
+        )
     for step in STEPS:
         greetings = greetings + jnp.where(below[step], 1, 0)
 
@@ -128,9 +142,6 @@
         for v in range(count_v)
         for m in range(here)
     ]
-    middle = jnp.logical_not(ends)
-    sends = [ends, place == 0]
-    passes = [middle, place == 1]
     always = far_copies[: len(far_copies) - ASIDE]
     moved = far_copies[: len(always) - 1 : -1]
     aside_copies = []
@@ -143,7 +154,7 @@
                 dst_ref=hop.at[piece],
                 send_sem=hop_sems.at[0, piece],
                 recv_sem=hop_sems.at[1, piece],
-                device_id=(inst, beside),
+                device_id=(inst, beside[piece]),
                 device_id_type=MESH,
             )
         )
@@ -153,7 +164,7 @@
                 dst_ref=far.at[m, v],
                 send_sem=hop_sems.at[2, piece],
                 recv_sem=far_recv.at[m, v],
-                device_id=(1 - inst, beside),
+                device_id=(1 - inst, beside[piece]),
                 device_id_type=MESH,
             )
         )
@@ -161,7 +172,9 @@
         copy.start()
     for step in STEPS:
         pl.when(below[step])(functools.partial(signal, ack.at[STEPS.index(-step)], at(step)))
-    pl.when((inst == 1) & ends)(functools.partial(signal, cross, (1 - inst, beside)))
+    pl.when(helps[1])(functools.partial(signal, helper, (inst, beside[1])))
+    for piece in range(ASIDE):
+        pl.when((inst == 1) & first)(functools.partial(signal, cross, (1 - inst, beside[piece])))
 
     for copy in local:
         copy.wait()
@@ -210,16 +223,35 @@
         )
         for step in STEPS
     ]
+    core = lax.rem(me, 2)
+    whole = {step: place >= 0 for step in STEPS}
+    whole[1] = jnp.logical_not((place == 3) & (core == 1))
+    whole[-1] = jnp.logical_not((place == 0) & (core == 0))
+    shares = ((place == 0) & (core == 1)) | ((place == 3) & (core == 0))
+    shared_copy = pltpu.make_async_remote_copy(
+        src_ref=rims.at[pl.ds(8 * (1 - core), 2)],
+        dst_ref=rims.at[pl.ds(6 - 4 * core, 2)],
+        send_sem=share_sem,
+        recv_sem=rim_recv.at[3 - 2 * core],
+        device_id=(inst, me + 1 - 2 * core),
+        device_id_type=MESH,
+    )
+
     def answered(step):
         pl.semaphore_wait(ack.at[STEPS.index(step)], 1)
-        rim_copies[STEPS.index(step)].start()
+        pl.when(whole[step])(rim_copies[STEPS.index(step)].start)
 
     for step, copy in zip(STEPS, rim_copies):
-        pl.when(below[step])(copy.start)
+        pl.when(below[step] & whole[step])(copy.start)
     for step in (1, 2):
         pl.when(above[step])(functools.partial(answered, step))
-    for piece in range(ASIDE):
-        pl.when(sends[piece])(aside_copies[piece].start)
+
+    @pl.when(first)
+    def _():
+        pl.semaphore_wait(helper, 1)
+        for copy in aside_copies:
+            copy.start()
+
     for copy in always[EARLY : len(always) - HELD]:
         copy.start()
 
@@ -233,22 +265,27 @@
 
     lax.fori_loop(0, count_v, own_source, 0)
 
-    pl.when(middle & (inst == 0))(functools.partial(pl.semaphore_wait, cross, 1))
+    pl.when((helps[0] | helps[1]) & (inst == 0))(functools.partial(pl.semaphore_wait, cross, 1))
 
     def pass_on(piece):
         aside_copies[piece].wait_recv()
         onward_copies[piece].start()
 
     for piece in range(ASIDE):
-        pl.when(passes[piece])(functools.partial(pass_on, piece))
+        pl.when(helps[piece])(functools.partial(pass_on, piece))
     for copy in always[len(always) - HELD :]:
         copy.start()
-    for piece in range(ASIDE):
-        pl.when(jnp.logical_not(sends[piece]))(moved[piece].start)
+    for copy in moved:
+        pl.when(jnp.logical_not(first))(copy.start)
     for step in (-1, -2):
         pl.when(above[step])(functools.partial(answered, step))
-    for copy in rim_copies:
-        copy.wait_recv()
+    two_back = rim_copies[STEPS.index(2)]
+    two_ahead = rim_copies[STEPS.index(-2)]
+    two_back.wait_recv()
+    two_ahead.wait_recv()
+    pl.when(shares)(shared_copy.start)
+    for step in (1, -1):
+        rim_copies[STEPS.index(step)].wait_recv()
     for face in range(2):
         picked = rims[picks[face]]
         amount = columns - shifts[face]
@@ -295,12 +332,15 @@
                 [spectral_weight(n - m - here, instances) for m in range(here)], values
             )
             out[n, v] = jnp.where(inside, out[n, v] - source, 0.0)
-    for copy in always + rim_copies:
+    for copy in always:
         copy.wait_send()
+    for step, copy in zip(STEPS, rim_copies):
+        pl.when(whole[step])(copy.wait_send)
+    pl.when(shares)(shared_copy.wait_send)
     for piece in range(ASIDE):
-        pl.when(sends[piece])(aside_copies[piece].wait_send)
-        pl.when(passes[piece])(onward_copies[piece].wait_send)
-        pl.when(jnp.logical_not(sends[piece]))(moved[piece].wait_send)
+        pl.when(first)(aside_copies[piece].wait_send)
+        pl.when(helps[piece])(onward_copies[piece].wait_send)
+        pl.when(jnp.logical_not(first))(moved[piece].wait_send)
 
 
 def on_device(state, slot_of, conn_block, conn_side, conn_shift, rows):
@@ -332,6 +372,8 @@
             pltpu.SemaphoreType.DMA((3, ASIDE)),
             pltpu.SemaphoreType.REGULAR((4,)),
             pltpu.SemaphoreType.REGULAR,
+            pltpu.SemaphoreType.REGULAR,
+            pltpu.SemaphoreType.DMA,
         ],
         compiler_params=pltpu.CompilerParams(
             collective_id=0, has_side_effects=True, vmem_limit_bytes=16 * 2**20

time: 40.2 us -> 38.8 us (0.965)
  the two profiles are of different devices: /device:TPU:466 before, /device:TPU:478 now
where the time goes in v5:
time: 38.8 us; the launch traced here: 38.7 us
  Pallas kernels  37.9 us (98%)
  local copies, waits for them, and re-layouts  0.84 us (2%)
    pallas_call x1, Pallas kernels, on_device(): pl.pallas_call(functools.partial(kernel, instances), out_shape=jax.ShapeD...  37.9 us
    unnamed x1, local copies, waits for them, and re-layouts  0.84 us

profile of v5, /device:TPU:478, one launch (start us, length us, event | category | flops | bytes accessed | tf_op | source)
XLA Modules:
  0.0 38.7 jit_solution(5750770125204408669)
XLA Ops:
  0.0 37.9 %residual.1 = f32[4,5,32,256]{3,2,1,0:T(8,128)S(1)} custom-call(f32[4,5,32,256]{3,2,1,0:T(8,128)} %bitcast.10, s32[1,256]{1,0:T(1,128)} %bitcast.14, s32[2,256]{1,0:T(2,128)} %bitcast.11, s32[2,256]{1,0:T(2,128)} %bitcast.12, s32[2,256]{1,0:T(2,128)} %bitcast.13, s32[1,256]{1,0:T(1,128)} %bitcast.15), custom_call_target="tpu_custom_call" | custom-call | tf_op jit(solution)/shard_map/residual/pallas_call | solution.py:351
  37.9 0.8 %copy.9 = f32[4,5,1,32,256]{4,3,2,1,0:T(8,128)} copy(f32[4,5,1,32,256]{4,3,2,1,0:T(8,128)S(1)} %bitcast.9) | data formatting | bytes 1310720

commit v6 on v5

--- a/solution.py
+++ b/solution.py
@@ -23,7 +23,7 @@
 
 def spectral_weight(offset, count):
     offset %= count
-    if offset == 0 or 2 * offset == count:
+    if offset == 0:
         return 0.0
     return 0.5 * FREQUENCY * (-1.0) ** offset / math.tan(math.pi * offset / count)
 
@@ -125,9 +125,6 @@
             ]
         )
     ]
-    for copy in local:
-        copy.start()
-
     pl.semaphore_wait(barrier, greetings)
 
     far_copies = [
@@ -169,6 +166,8 @@
             )
         )
     for copy in always[:EARLY]:
+        copy.start()
+    for copy in local:
         copy.start()
     for step in STEPS:
         pl.when(below[step])(functools.partial(signal, ack.at[STEPS.index(-step)], at(step)))

time: 38.8 us -> 38.8 us (level)
  no operation moved by 1% of the time
where the time goes in v6:
time: 38.8 us; the launch traced here: 38.7 us
  Pallas kernels  37.9 us (98%)
  local copies, waits for them, and re-layouts  0.84 us (2%)
    pallas_call x1, Pallas kernels, on_device(): pl.pallas_call(functools.partial(kernel, instances), out_shape=jax.ShapeD...  37.9 us
    unnamed x1, local copies, waits for them, and re-layouts  0.84 us

profile of v6, /device:TPU:478, one launch (start us, length us, event | category | flops | bytes accessed | tf_op | source)
XLA Modules:
  0.0 38.7 jit_solution(6900355224869924771)
XLA Ops:
  0.0 37.9 %residual.1 = f32[4,5,32,256]{3,2,1,0:T(8,128)S(1)} custom-call(f32[4,5,32,256]{3,2,1,0:T(8,128)} %bitcast.10, s32[1,256]{1,0:T(1,128)} %bitcast.14, s32[2,256]{1,0:T(2,128)} %bitcast.11, s32[2,256]{1,0:T(2,128)} %bitcast.12, s32[2,256]{1,0:T(2,128)} %bitcast.13, s32[1,256]{1,0:T(1,128)} %bitcast.15), custom_call_target="tpu_custom_call" | custom-call | tf_op jit(solution)/shard_map/residual/pallas_call | solution.py:350
  37.9 0.8 %copy.9 = f32[4,5,1,32,256]{4,3,2,1,0:T(8,128)} copy(f32[4,5,1,32,256]{4,3,2,1,0:T(8,128)S(1)} %bitcast.9) | data formatting | bytes 1310720

commit v7 on v6

--- a/solution.py
+++ b/solution.py
@@ -15,8 +15,8 @@
 MESH = pl.DeviceIdType.MESH
 OWN = REACH
 STEPS = (-2, 2, -1, 1)
-EARLY = 6
-HELD = 3
+EARLY = 9
+HELD = 5
 ASIDE = 2
 FIRST_ROW = 8
 

time: 38.8 us -> 38.8 us (level)
  no operation moved by 1% of the time
where the time goes in v7:
time: 38.8 us; the launch traced here: 38.7 us
  Pallas kernels  37.9 us (98%)
  local copies, waits for them, and re-layouts  0.84 us (2%)
    pallas_call x1, Pallas kernels, on_device(): pl.pallas_call(functools.partial(kernel, instances), out_shape=jax.ShapeD...  37.9 us
    unnamed x1, local copies, waits for them, and re-layouts  0.84 us

profile of v7, /device:TPU:478, one launch (start us, length us, event | category | flops | bytes accessed | tf_op | source)
XLA Modules:
  0.0 38.7 jit_solution(10839661505008921597)
XLA Ops:
  0.0 37.9 %residual.1 = f32[4,5,32,256]{3,2,1,0:T(8,128)S(1)} custom-call(f32[4,5,32,256]{3,2,1,0:T(8,128)} %bitcast.10, s32[1,256]{1,0:T(1,128)} %bitcast.14, s32[2,256]{1,0:T(2,128)} %bitcast.11, s32[2,256]{1,0:T(2,128)} %bitcast.12, s32[2,256]{1,0:T(2,128)} %bitcast.13, s32[1,256]{1,0:T(1,128)} %bitcast.15), custom_call_target="tpu_custom_call" | custom-call | tf_op jit(solution)/shard_map/residual/pallas_call | solution.py:350
  37.9 0.8 %copy.9 = f32[4,5,1,32,256]{4,3,2,1,0:T(8,128)} copy(f32[4,5,1,32,256]{4,3,2,1,0:T(8,128)S(1)} %bitcast.9) | data formatting | bytes 1310720
